TPU v7x, 32 devices: a whole 2x2x4 slice. The times are simulated.
32 devices in a mesh: exp: 8 (over y, x, core), seq: 4 (over z).
Axes of the slice: x: 2, y: 2, z: 4, core: 2. Of those that a mesh axis runs over, the one named last changes fastest.
Arguments:
- tokens: bfloat16 [8192, 768], P(('exp', 'seq')), may hold values from -6 to 6
- segments: int32 [8192], P('exp'), may hold values from 0 to 510, as said below
- expert_ids: int32 [8192, 2], P(('exp', 'seq')), may hold values from 0 to 15, all different within a row; in each aligned block of 256 rows (0 to 255, 256 to 511, ...) at most 39 rows name the same one
- gain_attn: bfloat16 [768], P(('exp', 'seq')), may hold values from 0.099609375 to 1.8984375
- attn_in: bfloat16 [768, 2304], P(('exp', 'seq')), may hold values from -0.21875 to 0.21875
- attn_out: bfloat16 [768, 768], P(('exp', 'seq')), may hold values from -1.75 to 1.75
- gain_ffn: bfloat16 [768], P(('exp', 'seq')), may hold values from 0.099609375 to 1.8984375
- router: bfloat16 [768, 16], P(('exp', 'seq')), may hold values from -0.15917969 to 0.15917969
- expert_in: bfloat16 [16, 768, 3072], P('exp', None, 'seq'), may hold values from -0.21875 to 0.21875
- expert_out: bfloat16 [16, 3072, 768], P('exp', 'seq'), may hold values from -0.15625 to 0.15625
- cotangent: bfloat16 [8192, 768], P(('exp', 'seq')), may hold values from -6 to 6
Outputs:
- mixed_out: bfloat16 [8192, 768], P(('exp', 'seq'))
- grad_tokens: float32 [8192, 768], P(('exp', 'seq'))
- grad_gain_attn: float32 [768], P(('exp', 'seq'))
- grad_attn_in: float32 [768, 2304], P(('exp', 'seq'))
- grad_attn_out: float32 [768, 768], P(('exp', 'seq'))
- grad_gain_ffn: float32 [768], P(('exp', 'seq'))
- grad_router: float32 [768, 16], P(('exp', 'seq'))
- grad_expert_in: float32 [16, 768, 3072], P('exp', None, 'seq')
- grad_expert_out: float32 [16, 3072, 768], P('exp', 'seq')
Inputs may be any that keep to these rules, and one draw needn't show every extreme that they name: `segments`: segment numbers never fall along a sequence of 1024 tokens and start at 0 in each sequence; in every draw some sequence reaches the largest number. `expert_ids`: each row names two different experts; among the rows of one device (256 aligned rows) no expert is named more than 39 times, and in some of these blocks one is named exactly 39 times.
All inputs are finite; a program needn't handle non-finite values.
Results may differ from a plain program's by a relative error of at most 0.014.
Values may be sent and summed in bfloat16 or wider, within the bound.
A program may use at most 256 MiB of HBM per device.

v0:
```python
import math

import jax
import jax.numpy as jnp
from jax import lax
from jax.sharding import PartitionSpec as P

HEAD_DIM = 64


EPSILON = 1e-06
MASKED = -1e30
HIGHEST = lax.Precision.HIGHEST


def contract_rows(first_operand, second_operand):
    return lax.dot_general(
        first_operand, second_operand, (((0,), (0,)), ((), ())), preferred_element_type=jnp.float32
    )


def contract_cols(first_operand, second_operand):
    return lax.dot_general(
        first_operand, second_operand, (((1,), (1,)), ((), ())), preferred_element_type=jnp.float32
    )


def norm_forward(values, gain_values):
    inverse = lax.rsqrt(jnp.mean(values * values, axis=-1, keepdims=True) + EPSILON)
    return (values * inverse * gain_values.astype(jnp.float32), inverse)


def norm_backward(values, inverse, gain_values, upstream):
    scaled = upstream * gain_values.astype(jnp.float32)
    gain_grad = jnp.sum(upstream * values * inverse, axis=0)
    value_grad = inverse * scaled - values * inverse**3 * jnp.mean(
        scaled * values, axis=-1, keepdims=True
    )
    return (value_grad, gain_grad)


def on_device(
    tokens,
    segments,
    expert_ids,
    gain_attn,
    attn_in,
    attn_out,
    gain_ffn,
    router,
    expert_in,
    expert_out,
    cotangent,
):
    tok_rows, model_width = tokens.shape
    head_count = model_width // HEAD_DIM
    score_scale = 1.0 / math.sqrt(HEAD_DIM)
    exp_size = lax.axis_size("exp")
    seq_index = lax.axis_index("seq")
    experts_dev = expert_in.shape[0]
    expert_total = router.shape[1]
    capacity = max(2, 5 * tok_rows // (2 * expert_total) - 1)
    buffer_rows = exp_size * capacity
    gain_one, w_qkv, w_output, gain_two, w_router = (
        lax.all_gather(gain_attn, ("exp", "seq"), axis=0, tiled=True),
        lax.all_gather(attn_in, ("exp", "seq"), axis=0, tiled=True),
        lax.all_gather(attn_out, ("exp", "seq"), axis=0, tiled=True),
        lax.all_gather(gain_ffn, ("exp", "seq"), axis=0, tiled=True),
        lax.all_gather(router, ("exp", "seq"), axis=0, tiled=True),
    )
    inputs = tokens.astype(jnp.float32)
    normed, inverse_one = norm_forward(inputs, gain_one)
    normed_low = normed.astype(jnp.bfloat16)
    qkv_low = jnp.dot(normed_low, w_qkv, preferred_element_type=jnp.float32).astype(jnp.bfloat16)
    queries = qkv_low[:, :model_width]
    key_values = lax.all_gather(qkv_low[:, model_width:], "seq", axis=0, tiled=True)
    total_keys = key_values.shape[0]
    query_place = seq_index * tok_rows + jnp.arange(tok_rows, dtype=jnp.int32)
    key_place = jnp.arange(total_keys, dtype=jnp.int32)
    query_segments = lax.dynamic_slice_in_dim(segments, seq_index * tok_rows, tok_rows)
    visible = (key_place[None, :] <= query_place[:, None]) & (
        segments[None, :] == query_segments[:, None]
    )
    head_outputs = []
    log_totals = []
    for head_index in range(head_count):
        first_col = head_index * HEAD_DIM
        query_head = queries[:, first_col : first_col + HEAD_DIM]
        key_head = key_values[:, first_col : first_col + HEAD_DIM]
        value_head = key_values[:, model_width + first_col : model_width + first_col + HEAD_DIM]
        scores = jnp.where(visible, contract_cols(query_head, key_head) * score_scale, MASKED)
        largest = jnp.max(scores, axis=1, keepdims=True)
        shifted = jnp.exp(scores - largest)
        totals = jnp.sum(shifted, axis=1, keepdims=True)
        weights_low = (shifted / totals).astype(jnp.bfloat16)
        head_outputs.append(jnp.dot(weights_low, value_head, preferred_element_type=jnp.float32))
        log_totals.append(largest + jnp.log(totals))
    attended_low = jnp.concatenate(head_outputs, axis=1).astype(jnp.bfloat16)
    hidden_state = inputs + jnp.dot(attended_low, w_output, preferred_element_type=jnp.float32)
    normed_two, inverse_two = norm_forward(hidden_state, gain_two)
    routed_low = normed_two.astype(jnp.bfloat16)
    logits = jnp.dot(routed_low, w_router, preferred_element_type=jnp.float32)
    chosen = (
        expert_ids[:, :, None] == jnp.arange(expert_total, dtype=jnp.int32)[None, None, :]
    ).astype(jnp.float32)
    picked = jnp.sum(chosen * logits[:, None, :], axis=2)
    gate_values = jax.nn.softmax(picked, axis=-1)
    flat_ids = expert_ids.reshape(-1)
    id_table = (flat_ids[:, None] == jnp.arange(expert_total, dtype=jnp.int32)[None, :]).astype(
        jnp.int32
    )
    slot_rank = jnp.sum((jnp.cumsum(id_table, axis=0) - id_table) * id_table, axis=1)
    position = (
        flat_ids // experts_dev * capacity + slot_rank
    ) * experts_dev + flat_ids % experts_dev
    send_rows = jnp.zeros((buffer_rows * experts_dev, model_width), jnp.bfloat16)
    send_rows = (
        send_rows.at[position]
        .set(jnp.repeat(routed_low, 2, axis=0))
        .reshape(buffer_rows, experts_dev, model_width)
    )
    received = lax.all_to_all(send_rows, "exp", split_axis=0, concat_axis=0, tiled=True)
    all_rows = lax.all_gather(received, "seq", axis=0, tiled=True)
    results = []
    for expert_local_expert in range(experts_dev):
        expert_pre_act = jnp.dot(
            all_rows[:, expert_local_expert],
            expert_in[expert_local_expert],
            preferred_element_type=jnp.float32,
        )
        hidden_low = jax.nn.gelu(expert_pre_act).astype(jnp.bfloat16)
        results.append(
            jnp.dot(hidden_low, expert_out[expert_local_expert], preferred_element_type=jnp.float32)
        )
    expert_result = lax.psum_scatter(
        jnp.stack(results, axis=1).astype(jnp.bfloat16), "seq", scatter_dimension=0, tiled=True
    )
    returned = lax.all_to_all(expert_result, "exp", split_axis=0, concat_axis=0, tiled=True)
    expert_values = returned.reshape(-1, model_width)[position].reshape(tok_rows, 2, model_width)
    expert_float = expert_values.astype(jnp.float32)
    mixed = hidden_state + jnp.sum(gate_values[:, :, None] * expert_float, axis=1)
    upstream = cotangent.astype(jnp.float32)
    gate_grad = jnp.sum(upstream[:, None, :] * expert_float, axis=2)
    picked_grad = gate_values * (
        gate_grad - jnp.sum(gate_values * gate_grad, axis=1, keepdims=True)
    )
    expert_grad_low = (gate_values[:, :, None] * upstream[:, None, :]).astype(jnp.bfloat16)
    logit_grad = jnp.sum(chosen * picked_grad[:, :, None], axis=1)
    router_grad = jnp.dot(routed_low.astype(jnp.float32).T, logit_grad, precision=HIGHEST)
    routed_grad = jnp.dot(logit_grad, w_router.astype(jnp.float32).T, precision=HIGHEST)
    send_grads = jnp.zeros((buffer_rows * experts_dev, model_width), jnp.bfloat16)
    send_grads = (
        send_grads.at[position]
        .set(expert_grad_low.reshape(-1, model_width))
        .reshape(buffer_rows, experts_dev, model_width)
    )
    grad_received = lax.all_to_all(send_grads, "exp", split_axis=0, concat_axis=0, tiled=True)
    in_grads = []
    out_grads = []
    grad_rows_all = lax.all_gather(grad_received, "seq", axis=0, tiled=True)
    pre_grads = []
    for local_expert in range(experts_dev):
        row_inputs = all_rows[:, local_expert]
        row_grads = grad_rows_all[:, local_expert]
        pre_act = jnp.dot(row_inputs, expert_in[local_expert], preferred_element_type=jnp.float32)
        activated, gelu_back = jax.vjp(jax.nn.gelu, pre_act)
        hidden_grad = contract_cols(row_grads, expert_out[local_expert])
        pre_low = gelu_back(hidden_grad)[0].astype(jnp.bfloat16)
        out_grads.append(contract_rows(activated.astype(jnp.bfloat16), row_grads))
        in_grads.append(contract_rows(row_inputs, pre_low))
        pre_grads.append(pre_low)
    results = []
    for local_expert in range(experts_dev):
        grad_piece = pre_grads[local_expert]
        results.append(contract_cols(grad_piece, expert_in[local_expert]))
    back_rows = lax.psum_scatter(
        jnp.stack(results, axis=1).astype(jnp.bfloat16), "seq", scatter_dimension=0, tiled=True
    ).astype(jnp.float32)
    grad_expert_in = jnp.stack(in_grads, axis=0)
    grad_expert_out = jnp.stack(out_grads, axis=0)
    grad_back = lax.all_to_all(
        back_rows.astype(jnp.bfloat16), "exp", split_axis=0, concat_axis=0, tiled=True
    ).astype(back_rows.dtype)
    routed_grad = routed_grad + jnp.sum(
        grad_back.reshape(-1, model_width)[position].reshape(tok_rows, 2, model_width), axis=1
    )
    state_grad, gain_two_grad = norm_backward(hidden_state, inverse_two, gain_two, routed_grad)
    state_grad = state_grad + upstream
    state_low = state_grad.astype(jnp.bfloat16)
    output_grad = contract_rows(attended_low, state_low)
    attended_grad = contract_cols(state_low, w_output).astype(jnp.bfloat16)
    query_grads = []
    key_parts = []
    value_parts = []
    for pair_index in range(head_count // 2):
        pieces_key = []
        pieces_value = []
        for head_index in (2 * pair_index, 2 * pair_index + 1):
            first_col = head_index * HEAD_DIM
            query_head = queries[:, first_col : first_col + HEAD_DIM]
            key_head = key_values[:, first_col : first_col + HEAD_DIM]
            value_head = key_values[:, model_width + first_col : model_width + first_col + HEAD_DIM]
            out_grad_head = attended_grad[:, first_col : first_col + HEAD_DIM]
            scores = contract_cols(query_head, key_head) * score_scale
            weights_full = jnp.where(visible, jnp.exp(scores - log_totals[head_index]), 0.0)
            weight_grad = contract_cols(out_grad_head, value_head)
            row_dot = jnp.sum(weights_full * weight_grad, axis=1, keepdims=True)
            score_low = (weights_full * (weight_grad - row_dot)).astype(jnp.bfloat16)
            query_grads.append(
                jnp.dot(score_low, key_head, preferred_element_type=jnp.float32) * score_scale
            )
            pieces_key.append(contract_rows(score_low, query_head) * score_scale)
            pieces_value.append(contract_rows(weights_full.astype(jnp.bfloat16), out_grad_head))
        own_block = lax.psum_scatter(
            jnp.concatenate(pieces_key + pieces_value, axis=1).astype(jnp.bfloat16),
            "seq",
            scatter_dimension=0,
            tiled=True,
        ).astype(jnp.float32)
        key_parts.append(own_block[:, : 2 * HEAD_DIM])
        value_parts.append(own_block[:, 2 * HEAD_DIM :])
    qkv_grad = jnp.concatenate(query_grads + key_parts + value_parts, axis=1).astype(jnp.bfloat16)
    weight_qkv_grad = contract_rows(normed_low, qkv_grad)
    normed_grad = contract_cols(qkv_grad, w_qkv)
    input_part, gain_one_grad = norm_backward(inputs, inverse_one, gain_one, normed_grad)
    input_grad = state_grad + input_part
    grads_own = (
        lax.psum_scatter(gain_one_grad, ("exp", "seq"), scatter_dimension=0, tiled=True),
        lax.psum_scatter(weight_qkv_grad, ("exp", "seq"), scatter_dimension=0, tiled=True),
        lax.psum_scatter(output_grad, ("exp", "seq"), scatter_dimension=0, tiled=True),
        lax.psum_scatter(gain_two_grad, ("exp", "seq"), scatter_dimension=0, tiled=True),
        lax.psum_scatter(router_grad, ("exp", "seq"), scatter_dimension=0, tiled=True),
    )
    return (
        mixed.astype(jnp.bfloat16),
        input_grad,
        grads_own[0],
        grads_own[1],
        grads_own[2],
        grads_own[3],
        grads_own[4],
        grad_expert_in,
        grad_expert_out,
    )


def solution(mesh):
    return jax.shard_map(
        on_device,
        mesh=mesh,
        in_specs=(
            P(("exp", "seq"), None),
            P("exp"),
            P(("exp", "seq"), None),
            P(("exp", "seq")),
            P(("exp", "seq"), None),
            P(("exp", "seq"), None),
            P(("exp", "seq")),
            P(("exp", "seq"), None),
            P("exp", None, "seq"),
            P("exp", "seq", None),
            P(("exp", "seq"), None),
        ),
        out_specs=(
            P(("exp", "seq"), None),
            P(("exp", "seq"), None),
            P(("exp", "seq")),
            P(("exp", "seq"), None),
            P(("exp", "seq"), None),
            P(("exp", "seq")),
            P(("exp", "seq"), None),
            P("exp", None, "seq"),
            P("exp", "seq", None),
        ),
        check_vma=False,
    )
```

profile of v0, /device:TPU:0, one launch (start us, length us, event | category | flops | bytes accessed | tf_op | source)
XLA Modules:
  0.0 960.8 jit_solution(2483141225691717377)
XLA Ops:
  9.7 42.0 %all-reduce.6 = (bf16[768]{0:T(1024)(128)(2,1)S(1)}, bf16[768]{0:T(1024)(128)(2,1)S(1)}) all-reduce(bf16[768]{0:T(1024)(128)(2,1)S(1)} %dynamic-update-slice, bf16[768]{0:T(1024)(128)(2,1)S(1)} %dynamic-update-slice.1), channel_id=1, replica_groups=mesh['exp'=8,'seq'=4] {'exp','seq'}, use_global_device_ids=true, to_apply=%add | all-reduce | flops 1536 | bytes 6144
  53.5 20.3 %all-gather.7.cloned.1.call-done = bf16[768,2304]{1,0:T(8,128)(2,1)} async-done(((bf16[24,2304]{1,0:T(8,128)(2,1)}), bf16[768,2304]{1,0:T(8,128)(2,1)}) %all-gather.7.cloned.1.call-update) | async-done | bytes 3538960 | tf_op jit(solution)/shard_map/all_gather | solution.py:66
  73.8 3.3 convolution_convert_fusion
  81.1 59.4 %all-gather.9.cloned.1.call-done = bf16[1024,1536]{1,0:T(8,128)(2,1)} async-done(((bf16[256,1536]{1,0:T(8,128)(2,1)}), bf16[1024,1536]{1,0:T(8,128)(2,1)}) %all-gather.9.cloned.1.call-update) | async-done | bytes 3145744 | tf_op jit(solution)/shard_map/all_gather | solution.py:76
  150.6 2.4 fusion.101
  161.7 34.6 %all-gather.11.cloned.1.call-done = bf16[768,768]{1,0:T(8,128)(2,1)} async-done(((bf16[24,768]{1,0:T(8,128)(2,1)}), bf16[768,768]{1,0:T(8,128)(2,1)}) %all-gather.11.cloned.1.call-update) | async-done | bytes 1179664 | tf_op jit(solution)/shard_map/all_gather | solution.py:67
  199.6 2.9 scatter_custom_fusion
  202.9 17.6 %all_to_all.20 = bf16[312,2,768]{2,1,0:T(2,128)(2,1)} all-to-all(bf16[312,2,768]{2,1,0:T(2,128)(2,1)S(1)} %reshape.470), channel_id=1, replica_groups=mesh['exp'=8,'seq'=4] {'exp'}, dimensions={0} | all-to-all | bytes 1916928 | tf_op jit(solution)/shard_map/all_to_all | solution.py:122
  220.7 68.4 %all-gather = bf16[32,24,16]{1,2,0:T(8,128)(2,1)S(1)} all-gather(bf16[1,24,16]{1,2,0:T(8,128)(2,1)S(1)} %bitcast.140), channel_id=1, replica_groups=mesh['exp'=8,'seq'=4] {'exp','seq'}, dimensions={0}, use_global_device_ids=true | all-gather | bytes 25344 | tf_op jit(solution)/shard_map/all_gather | solution.py:69
  290.9 12.6 %mul.535 = f32[512,768]{1,0:T(8,128)S(1)} reshape(f32[256,2,768]{2,1,0:T(2,128)} %mul.528) | data formatting | bytes 3145728 | tf_op jit(solution)/shard_map/mul | solution.py:143
  304.2 3.7 scatter_custom_fusion.1
  307.9 2.4 reshape.472
  310.3 17.5 %all_to_all.21 = bf16[312,2,768]{2,1,0:T(2,128)(2,1)} all-to-all(bf16[312,2,768]{2,1,0:T(2,128)(2,1)S(1)} %reshape.472), channel_id=1, replica_groups=mesh['exp'=8,'seq'=4] {'exp'}, dimensions={0} | all-to-all | bytes 1916928 | tf_op jit(solution)/shard_map/all_to_all | solution.py:157
  327.9 8.4 fusion.299
  341.8 2.4 fusion.14
  344.3 2.4 fusion.15
  349.3 49.9 %all-gather.15.cloned.1.call-done = bf16[1248,2,768]{2,1,0:T(2,128)(2,1)} async-done(((bf16[312,2,768]{2,1,0:T(2,128)(2,1)}), bf16[1248,2,768]{2,1,0:T(2,128)(2,1)}) %all-gather.15.cloned.1.call-update) | async-done | bytes 3833872 | tf_op jit(solution)/shard_map/all_gather | solution.py:160
  399.1 8.6 fusion.298
  407.8 3.8 fusion.6
  414.4 3.7 fusion.13
  427.1 44.0 %reduce-scatter.32.cloned.1.call-done = bf16[312,1536]{1,0:T(8,128)(2,1)} async-done(((bf16[1248,1536]{1,0:T(8,128)(2,1)}), bf16[312,1536]{1,0:T(8,128)(2,1)}) %reduce-scatter.32.cloned.1.call-update) | async-done | bytes 958480
  471.0 3.3 reshape.518
  474.3 3.8 all-to-all-start.1
  480.5 64.4 %reduce-scatter.34.cloned.1.call-done = bf16[312,1536]{1,0:T(8,128)(2,1)} async-done(((bf16[1248,1536]{1,0:T(8,128)(2,1)}), bf16[312,1536]{1,0:T(8,128)(2,1)}) %reduce-scatter.34.cloned.1.call-update) | async-done | bytes 958480
  544.9 3.3 reshape.520
  548.2 4.2 all-to-all-start.3
  553.9 2.7 gather_fusion
  558.7 4.9 multiply_reduce_fusion
  563.8 3.1 all-to-all-done.3
  566.9 2.4 reshape.478
  569.3 2.8 gather_fusion.1
  572.1 2.4 reshape.475
  574.5 2.9 reduce_sum.366
  599.9 3.3 multiply_reduce_fusion.3
  603.3 2.5 multiply_convert_fusion.4
  619.8 2.8 multiply_reduce_fusion.4
  622.6 3.2 multiply_convert_fusion.5
  645.2 3.2 fusion.201
  669.5 11.7 %reduce-scatter.22.cloned.1.call-done = bf16[256,256]{0,1:T(8,128)(2,1)} async-done(((bf16[1024,256]{0,1:T(8,128)(2,1)}), bf16[256,256]{0,1:T(8,128)(2,1)}) %reduce-scatter.22.cloned.1.call-update) | async-done | bytes 131088 | tf_op jit(solution)/shard_map/reduce_scatter | solution.py:214
  682.6 20.6 %reduce-scatter.24.cloned.1.call-done = bf16[256,256]{0,1:T(8,128)(2,1)} async-done(((bf16[1024,256]{0,1:T(8,128)(2,1)}), bf16[256,256]{0,1:T(8,128)(2,1)}) %reduce-scatter.24.cloned.1.call-update) | async-done | bytes 131088 | tf_op jit(solution)/shard_map/reduce_scatter | solution.py:214
  704.7 20.7 %reduce-scatter.26.cloned.1.call-done = bf16[256,256]{0,1:T(8,128)(2,1)} async-done(((bf16[1024,256]{0,1:T(8,128)(2,1)}), bf16[256,256]{0,1:T(8,128)(2,1)}) %reduce-scatter.26.cloned.1.call-update) | async-done | bytes 131088 | tf_op jit(solution)/shard_map/reduce_scatter | solution.py:214
  735.7 5.4 fusion.204
  742.6 4.1 convolution_bitcast_fusion.3
  755.7 4.7 pad_maximum_fusion
  760.7 2.6 fusion.112
  763.3 39.4 %all-reduce.5 = (f32[768]{0:T(1024)S(1)}, f32[768]{0:T(1024)S(1)}, f32[768,16]{0,1:T(8,128)S(1)}) all-reduce(f32[768]{0:T(1024)S(1)} %get-tuple-element.13, f32[768]{0:T(1024)S(1)} %get-tuple-element.9, f32[768,16]{0,1:T(8,128)S(1)} %fusion.301), channel_id=10, replica_groups=mesh['exp'=8,'seq'=4] {'exp','seq'}, use_global_device_ids=true, to_apply=%region_62.63.clone | all-reduce | flops 13824 | bytes 110592
  805.7 22.8 %reduce-scatter.30.cloned.1.call-done = f32[24,768]{1,0:T(8,128)} async-done(((f32[768,768]{1,0:T(8,128)}), f32[24,768]{1,0:T(8,128)}) %reduce-scatter.30.cloned.1.call-update) | async-done | bytes 73744 | tf_op jit(solution)/shard_map/reduce_scatter | solution.py:230
  828.5 125.2 %reduce-scatter.28.cloned.1.call-done = f32[24,2304]{1,0:T(8,128)} async-done(((f32[768,2304]{1,0:T(8,128)}), f32[24,2304]{1,0:T(8,128)}) %reduce-scatter.28.cloned.1.call-update) | async-done | bytes 221200 | tf_op jit(solution)/shard_map/reduce_scatter | solution.py:229
  (523 shorter events, 161.2 us)
Async XLA Ops:
  7.2 66.6 %all-gather.7.cloned.1.call-start = ((), (), s32[]{:S(2)}) async-start(), calls=%async_computation.14 | async-start | bytes 3649536 | tf_op jit(solution)/shard_map/all_gather | solution.py:66
  7.9 132.6 %all-gather.9.cloned.1.call-start = ((), (), s32[]{:S(2)}) async-start(), calls=%async_computation.15 | async-start | bytes 3932160 | tf_op jit(solution)/shard_map/all_gather | solution.py:76
  51.7 26.4 %copy-start.73 = (f32[768]{0:T(1024)}, f32[768]{0:T(1024)S(1)}, u32[]{:S(2)}) copy-start(f32[768]{0:T(1024)S(1)} %convert_element_type.198) | copy-start | bytes 9220
  53.5 24.6 %copy-start.78 = (f32[256]{0:T(256)}, f32[256]{0:T(256)S(1)}, u32[]{:S(2)}) copy-start(f32[256]{0:T(256)S(1)} %get-tuple-element.75) | copy-start | bytes 3076
  77.1 71.1 %copy-start.58 = (bf16[256,2304]{1,0:T(8,128)(2,1)}, bf16[256,2304]{1,0:T(8,128)(2,1)S(1)}, u32[]{:S(2)}) copy-start(bf16[256,2304]{1,0:T(8,128)(2,1)S(1)} %convolution_convert_fusion) | copy-start | bytes 3538948
  78.1 118.2 %all-gather.11.cloned.1.call-start = ((), (), s32[]{:S(2)}) async-start(), calls=%async_computation.16 | async-start | bytes 1216512 | tf_op jit(solution)/shard_map/all_gather | solution.py:67
  78.8 249.1 %all-gather.13.cloned.1.call-start = ((), (), s32[]{:S(2)}) async-start(), calls=%async_computation.17 | async-start | bytes 4792320 | tf_op jit(solution)/shard_map/all_gather | solution.py:123
  81.1 118.5 %copy-start.113 = (s32[512,1]{0,1:T(1,128)}, s32[512,1]{0,1:T(1,128)S(1)}, u32[]{:S(2)}) copy-start(s32[512,1]{0,1:T(1,128)S(1)} %compare_select_fusion) | copy-start | bytes 6148
  142.0 18.4 %copy-start.2 = (f32[256,1024]{1,0:T(8,128)}, f32[256,1024]{1,0:T(8,128)S(1)}, u32[]{:S(2)}) copy-start(f32[256,1024]{1,0:T(8,128)S(1)} %convolution_multiply_fusion.1) | copy-start | bytes 3145732
  161.0 35.3 %copy-start.40 = (bf16[256,768]{1,0:T(8,128)(2,1)S(1)}, bf16[256,768]{1,0:T(8,128)(2,1)}, u32[]{:S(2)}) copy-start(bf16[256,768]{1,0:T(8,128)(2,1)} %param.11) | copy-start | bytes 1179652
  161.7 37.1 %copy-start.69 = (bf16[256,768]{0,1:T(8,128)(2,1)}, bf16[256,768]{0,1:T(8,128)(2,1)S(1)}, u32[]{:S(2)}) copy-start(bf16[256,768]{0,1:T(8,128)(2,1)S(1)} %fusion.70) | copy-start | bytes 1179652
  198.9 104.7 %copy-start.41 = (bf16[256,768]{1,0:T(8,128)(2,1)}, bf16[256,768]{1,0:T(8,128)(2,1)S(1)}, u32[]{:S(2)}) copy-start(bf16[256,768]{1,0:T(8,128)(2,1)S(1)} %multiply_convert_fusion.16) | copy-start | bytes 1179652
  199.6 21.1 %copy-start.145 = (bf16[24,16]{0,1:T(8,128)(2,1)S(1)}, bf16[24,16]{0,1:T(8,128)(2,1)}, u32[]{:S(2)}) copy-start(bf16[24,16]{0,1:T(8,128)(2,1)} %param.18) | copy-start | bytes 2308
  202.9 86.4 %copy-start.66 = (bf16[256,768]{1,0:T(8,128)(2,1)S(1)}, bf16[256,768]{1,0:T(8,128)(2,1)}, u32[]{:S(2)}) copy-start(bf16[256,768]{1,0:T(8,128)(2,1)} %param.21) | copy-start | bytes 1179652
  220.6 178.5 %all-gather.15.cloned.1.call-start = ((), (), s32[]{:S(2)}) async-start(), calls=%async_computation.18 | async-start | bytes 4792320 | tf_op jit(solution)/shard_map/all_gather | solution.py:160
  304.0 23.8 %copy-start.70 = (f32[256,2]{1,0:T(8,128)}, f32[256,2]{1,0:T(8,128)S(1)}, u32[]{:S(2)}) copy-start(f32[256,2]{1,0:T(8,128)S(1)} %copy.67) | copy-start | bytes 6148
  327.8 143.2 %reduce-scatter.32.cloned.1.call-start = ((), (), s32[]{:S(2)}) async-start(), calls=%async_computation.27 | async-start | bytes 4792320
  349.2 195.7 %reduce-scatter.34.cloned.1.call-start = ((), (), s32[]{:S(2)}) async-start(), calls=%async_computation.28 | async-start | bytes 4792320
  424.8 53.3 %copy-start.88 = (f32[256]{0:T(256)S(1)}, f32[256]{0:T(256)}, u32[]{:S(2)}) copy-start(f32[256]{0:T(256)} %copy-done.87) | copy-start | bytes 3076
  424.8 53.3 %copy-start.124 = (f32[256]{0:T(256)S(1)}, f32[256]{0:T(256)}, u32[]{:S(2)}) copy-start(f32[256]{0:T(256)} %copy-done.123) | copy-start | bytes 3076
  424.8 53.9 %copy-start.96 = (f32[256]{0:T(256)S(1)}, f32[256]{0:T(256)}, u32[]{:S(2)}) copy-start(f32[256]{0:T(256)} %copy-done.95) | copy-start | bytes 3076
  424.8 53.9 %copy-start.98 = (f32[256]{0:T(256)S(1)}, f32[256]{0:T(256)}, u32[]{:S(2)}) copy-start(f32[256]{0:T(256)} %copy-done.97) | copy-start | bytes 3076
  424.8 53.9 %copy-start.132 = (f32[256]{0:T(256)S(1)}, f32[256]{0:T(256)}, u32[]{:S(2)}) copy-start(f32[256]{0:T(256)} %copy-done.131) | copy-start | bytes 3076
  424.8 53.9 %copy-start.134 = (f32[256]{0:T(256)S(1)}, f32[256]{0:T(256)}, u32[]{:S(2)}) copy-start(f32[256]{0:T(256)} %copy-done.133) | copy-start | bytes 3076
  424.8 54.5 %copy-start.92 = (f32[256]{0:T(256)S(1)}, f32[256]{0:T(256)}, u32[]{:S(2)}) copy-start(f32[256]{0:T(256)} %copy-done.91) | copy-start | bytes 3076
  424.8 54.5 %copy-start.94 = (f32[256]{0:T(256)S(1)}, f32[256]{0:T(256)}, u32[]{:S(2)}) copy-start(f32[256]{0:T(256)} %copy-done.93) | copy-start | bytes 3076
  424.8 54.5 %copy-start.128 = (f32[256]{0:T(256)S(1)}, f32[256]{0:T(256)}, u32[]{:S(2)}) copy-start(f32[256]{0:T(256)} %copy-done.127) | copy-start | bytes 3076
  424.8 54.5 %copy-start.130 = (f32[256]{0:T(256)S(1)}, f32[256]{0:T(256)}, u32[]{:S(2)}) copy-start(f32[256]{0:T(256)} %copy-done.129) | copy-start | bytes 3076
  424.8 55.1 %copy-start.90 = (f32[256]{0:T(256)S(1)}, f32[256]{0:T(256)}, u32[]{:S(2)}) copy-start(f32[256]{0:T(256)} %copy-done.89) | copy-start | bytes 3076
  424.9 55.1 %copy-start.116 = (f32[256]{0:T(256)S(1)}, f32[256]{0:T(256)}, u32[]{:S(2)}) copy-start(f32[256]{0:T(256)} %copy-done.115) | copy-start | bytes 3076
  424.9 55.1 %copy-start.126 = (f32[256]{0:T(256)S(1)}, f32[256]{0:T(256)}, u32[]{:S(2)}) copy-start(f32[256]{0:T(256)} %copy-done.125) | copy-start | bytes 3076
  425.9 128.0 %copy-start.82 = (s32[1024]{0:T(1024)}, s32[1024]{0:T(1024)S(1)}, u32[]{:S(2)}) copy-start(s32[1024]{0:T(1024)S(1)} %pad_clamp_fusion) | copy-start | bytes 12292
  474.3 78.6 %copy-start.86 = (f32[256]{0:T(256)S(1)}, f32[256]{0:T(256)}, u32[]{:S(2)}) copy-start(f32[256]{0:T(256)} %copy-done.85) | copy-start | bytes 3076
  474.3 78.6 %copy-start.122 = (f32[256]{0:T(256)S(1)}, f32[256]{0:T(256)}, u32[]{:S(2)}) copy-start(f32[256]{0:T(256)} %copy-done.121) | copy-start | bytes 3076
  474.3 73.9 %all-to-all-start.1 = ((bf16[312,2,768]{2,1,0:T(2,128)(2,1)}), bf16[312,2,768]{2,1,0:T(2,128)(2,1)S(1)}, u32[]{:S(2)}, u32[]{:S(2)}) async-start(bf16[312,2,768]{2,1,0:T(2,128)(2,1)} %reshape.518), calls=%async_computation.1 | async-start | bytes 1916928 | tf_op jit(solution)/shard_map/all_to_all | solution.py:138
  548.2 18.7 %all-to-all-start.3 = ((bf16[312,2,768]{2,1,0:T(2,128)(2,1)}), bf16[312,2,768]{2,1,0:T(2,128)(2,1)}, u32[]{:S(2)}, u32[]{:S(2)}) async-start(bf16[312,2,768]{2,1,0:T(2,128)(2,1)} %reshape.520), calls=%async_computation.3 | async-start | bytes 1916928 | tf_op jit(solution)/shard_map/all_to_all | solution.py:181
  552.4 112.6 %reduce-scatter.16.cloned.1.call-start = ((), (), s32[]{:S(2)}) async-start(), calls=%async_computation.19 | async-start | bytes 655360 | tf_op jit(solution)/shard_map/reduce_scatter | solution.py:214
  594.1 72.4 %reduce-scatter.18.cloned.1.call-start = ((), (), s32[]{:S(2)}) async-start(), calls=%async_computation.20 | async-start | bytes 655360 | tf_op jit(solution)/shard_map/reduce_scatter | solution.py:214
  611.6 56.4 %reduce-scatter.20.cloned.1.call-start = ((), (), s32[]{:S(2)}) async-start(), calls=%async_computation.21 | async-start | bytes 655360 | tf_op jit(solution)/shard_map/reduce_scatter | solution.py:214
  618.4 62.7 %reduce-scatter.22.cloned.1.call-start = ((), (), s32[]{:S(2)}) async-start(), calls=%async_computation.22 | async-start | bytes 655360 | tf_op jit(solution)/shard_map/reduce_scatter | solution.py:214
  631.7 71.5 %reduce-scatter.24.cloned.1.call-start = ((), (), s32[]{:S(2)}) async-start(), calls=%async_computation.23 | async-start | bytes 655360 | tf_op jit(solution)/shard_map/reduce_scatter | solution.py:214
  638.4 87.0 %reduce-scatter.26.cloned.1.call-start = ((), (), s32[]{:S(2)}) async-start(), calls=%async_computation.24 | async-start | bytes 655360 | tf_op jit(solution)/shard_map/reduce_scatter | solution.py:214
  645.2 183.3 %reduce-scatter.30.cloned.1.call-start = ((), (), s32[]{:S(2)}) async-start(), calls=%async_computation.26 | async-start | bytes 2433024 | tf_op jit(solution)/shard_map/reduce_scatter | solution.py:230
  648.4 305.3 %reduce-scatter.28.cloned.1.call-start = ((), (), s32[]{:S(2)}) async-start(), calls=%async_computation.25 | async-start | bytes 7299072 | tf_op jit(solution)/shard_map/reduce_scatter | solution.py:229
  659.1 76.5 %copy-start.74 = (f32[768]{0:T(1024)S(1)}, f32[768]{0:T(1024)}, u32[]{:S(2)}) copy-start(f32[768]{0:T(1024)} %copy-done.73) | copy-start | bytes 9220
  659.1 76.5 %copy-start.79 = (f32[256]{0:T(256)S(1)}, f32[256]{0:T(256)}, u32[]{:S(2)}) copy-start(f32[256]{0:T(256)} %copy-done.78) | copy-start | bytes 3076
  760.6 43.9 %copy-start.31 = (f32[256,768]{1,0:T(8,128)S(1)}, f32[256,768]{1,0:T(8,128)}, u32[]{:S(2)}) copy-start(f32[256,768]{1,0:T(8,128)} %copy-done.30) | copy-start | bytes 2359300
  760.7 43.9 %copy-start.119 = (f32[256]{0:T(256)S(1)}, f32[256]{0:T(256)}, u32[]{:S(2)}) copy-start(f32[256]{0:T(256)} %get-tuple-element.74) | copy-start | bytes 3076
  (131 other events, 670.2 us)
Sparse Core Ops, SparseCore 0:
  10.8 62.9 all-gather.6
  78.2 62.2 all-gather.8
  143.4 52.8 all-gather.10
  220.7 74.7 all-gather.12
  328.0 71.1 all-gather.14
  401.3 69.6 reduce-scatter.31
  473.5 71.3 reduce-scatter.33
  594.3 20.2 reduce-scatter.15
  616.8 19.8 reduce-scatter.17
  638.8 19.9 reduce-scatter.19
  661.0 20.0 reduce-scatter.21
  683.2 19.9 reduce-scatter.23
  705.5 19.8 reduce-scatter.25
  731.1 97.3 reduce-scatter.29
  835.5 118.1 reduce-scatter.27
where the time goes:
time: 971 us; the launch traced here: 961 us
  waiting for transfers between devices  478 us (49%)
  blocking collectives  185 us (19%)
  matrix products  129 us (13%)
  local copies, waits for them, and re-layouts  96.9 us (10%)
  other arithmetic  45.3 us (5%)
  between operations  16.8 us (2%)
    reduce_scatter x1, waiting for transfers between devices, on_device(): lax.psum_scatter(weight_qkv_grad, ('exp', 'seq'), scatter_dimension=0, ti...  125 us
    unnamed x17, waiting for transfers between devices  110 us
    unnamed x2, blocking collectives  81.5 us
    all_gather x1, blocking collectives, on_device(): lax.all_gather(router, ('exp', 'seq'), axis=0, tiled=True)  68.4 us
    all_gather x1, waiting for transfers between devices, on_device(): lax.all_gather(qkv_low[:, model_width:], 'seq', axis=0, tiled=True)  59.4 us
    reduce_scatter x6, waiting for transfers between devices, on_device(): lax.psum_scatter(jnp.concatenate(pieces_key + pieces_value, axis=1).astyp...  53 us
    all_gather x1, waiting for transfers between devices, on_device(): grad_rows_all = lax.all_gather(grad_received, 'seq', axis=0, tiled=True)  49.9 us
    dot_general x30, matrix products, contract_rows(): lax.dot_general(first_operand, second_operand, (((0,), (0,)), ((), ())),...  49.4 us
  transfers between devices with their start and end apart: 17, of which 12 were waited for; matrix products, arithmetic and copies ran while one was open for 23% of the time, Pallas kernels for 0%

commit v1 on v0

v1 whole, which is shorter than its diff:
```python
import math

import jax
import jax.numpy as jnp
from jax import lax
from jax.experimental import pallas as pl
from jax.experimental.pallas import tpu as pltpu
from jax.sharding import PartitionSpec as P

HEAD_DIM = 64


EPSILON = 1e-06
MASKED = -1e30
HIGHEST = lax.Precision.HIGHEST


def contract_rows(first_operand, second_operand):
    return lax.dot_general(
        first_operand, second_operand, (((0,), (0,)), ((), ())), preferred_element_type=jnp.float32
    )


def contract_cols(first_operand, second_operand):
    return lax.dot_general(
        first_operand, second_operand, (((1,), (1,)), ((), ())), preferred_element_type=jnp.float32
    )


def norm_forward(values, gain_values):
    inverse = lax.rsqrt(jnp.mean(values * values, axis=-1, keepdims=True) + EPSILON)
    return (values * inverse * gain_values.astype(jnp.float32), inverse)


def norm_backward(values, inverse, gain_values, upstream):
    scaled = upstream * gain_values.astype(jnp.float32)
    gain_grad = jnp.sum(upstream * values * inverse, axis=0)
    value_grad = inverse * scaled - values * inverse**3 * jnp.mean(
        scaled * values, axis=-1, keepdims=True
    )
    return (value_grad, gain_grad)


BLOCK_ROWS = 256
VMEM_BYTES = 40 * 1024 * 1024


def head_softmax(qkv_ref, col_ref, row_ref, own_cols, head_index, first_row, rows):
    stop = first_row + rows
    first_col = head_index * HEAD_DIM
    query = qkv_ref[first_row:stop, first_col : first_col + HEAD_DIM]
    key = qkv_ref[0:stop, own_cols + first_col : own_cols + first_col + HEAD_DIM]
    value = qkv_ref[0:stop, 2 * own_cols + first_col : 2 * own_cols + first_col + HEAD_DIM]
    query_place = first_row + lax.broadcasted_iota(jnp.int32, (rows, stop), 0)
    key_place = lax.broadcasted_iota(jnp.int32, (rows, stop), 1)
    visible = (key_place <= query_place) & (col_ref[first_row:stop, :] == row_ref[:, 0:stop])
    scores = contract_cols(query, key) * (1.0 / math.sqrt(HEAD_DIM))
    scores = jnp.where(visible, scores, MASKED)
    shifted = jnp.exp(scores - jnp.max(scores, axis=1, keepdims=True))
    weights = shifted / jnp.sum(shifted, axis=1, keepdims=True)
    return query, key, value, weights


def attend_kernel(qkv_ref, col_ref, row_ref, out_ref):
    own_cols = out_ref.shape[1]
    rows = min(BLOCK_ROWS, out_ref.shape[0])
    for first_row in range(0, out_ref.shape[0], rows):
        pieces = []
        for head_index in range(own_cols // HEAD_DIM):
            _, _, value, weights = head_softmax(
                qkv_ref, col_ref, row_ref, own_cols, head_index, first_row, rows
            )
            pieces.append(
                jnp.dot(weights.astype(jnp.bfloat16), value, preferred_element_type=jnp.float32)
            )
        out_ref[first_row : first_row + rows, :] = jnp.concatenate(pieces, axis=1).astype(
            jnp.bfloat16
        )


def attend_back_kernel(qkv_ref, grad_ref, col_ref, row_ref, out_ref, key_sum, value_sum):
    own_cols = grad_ref.shape[1]
    heads = own_cols // HEAD_DIM
    total = grad_ref.shape[0]
    rows = min(BLOCK_ROWS, total)
    scale = 1.0 / math.sqrt(HEAD_DIM)
    key_sum[...] = jnp.zeros_like(key_sum)
    value_sum[...] = jnp.zeros_like(value_sum)
    for first_row in range(0, total, rows):
        stop = first_row + rows
        pieces = []
        for head_index in range(heads):
            query, key, value, weights = head_softmax(
                qkv_ref, col_ref, row_ref, own_cols, head_index, first_row, rows
            )
            first_col = head_index * HEAD_DIM
            out_grad = grad_ref[first_row:stop, first_col : first_col + HEAD_DIM]
            weight_grad = contract_cols(out_grad, value)
            row_dot = jnp.sum(weights * weight_grad, axis=1, keepdims=True)
            score_low = (weights * (weight_grad - row_dot)).astype(jnp.bfloat16)
            pieces.append(jnp.dot(score_low, key, preferred_element_type=jnp.float32) * scale)
            key_sum[head_index, 0:stop, :] += contract_rows(score_low, query)
            value_sum[head_index, 0:stop, :] += contract_rows(
                weights.astype(jnp.bfloat16), out_grad
            )
        out_ref[first_row:stop, 0:own_cols] = jnp.concatenate(pieces, axis=1).astype(jnp.bfloat16)
    sums = [key_sum[n] * scale for n in range(heads)] + [value_sum[n] for n in range(heads)]
    out_ref[:, own_cols : 3 * own_cols] = jnp.concatenate(sums, axis=1).astype(jnp.bfloat16)


def attend(qkv_own, segments):
    total, width = qkv_own.shape
    return pl.pallas_call(
        attend_kernel,
        out_shape=jax.ShapeDtypeStruct((total, width // 3), jnp.bfloat16),
        compiler_params=pltpu.CompilerParams(vmem_limit_bytes=VMEM_BYTES),
        cost_estimate=pl.CostEstimate(
            flops=total * total * width, bytes_accessed=4 * total * width, transcendentals=0
        ),
    )(qkv_own, segments[:, None], segments[None, :])


def attend_back(qkv_own, attended_grad, segments):
    total, width = qkv_own.shape
    heads = width // (3 * HEAD_DIM)
    return pl.pallas_call(
        attend_back_kernel,
        out_shape=jax.ShapeDtypeStruct((total, width), jnp.bfloat16),
        scratch_shapes=[
            pltpu.VMEM((heads, total, HEAD_DIM), jnp.float32),
            pltpu.VMEM((heads, total, HEAD_DIM), jnp.float32),
        ],
        compiler_params=pltpu.CompilerParams(vmem_limit_bytes=VMEM_BYTES),
        cost_estimate=pl.CostEstimate(
            flops=3 * total * total * width, bytes_accessed=6 * total * width, transcendentals=0
        ),
    )(qkv_own, attended_grad, segments[:, None], segments[None, :])


def on_device(
    tokens,
    segments,
    expert_ids,
    gain_attn,
    attn_in,
    attn_out,
    gain_ffn,
    router,
    expert_in,
    expert_out,
    cotangent,
):
    tok_rows, model_width = tokens.shape
    head_count = model_width // HEAD_DIM
    exp_size = lax.axis_size("exp")
    seq_size = lax.axis_size("seq")
    seq_index = lax.axis_index("seq")
    exp_index = lax.axis_index("exp")
    experts_dev = expert_in.shape[0]
    expert_total = router.shape[1]
    own_rows = attn_in.shape[0]
    capacity = max(2, 5 * tok_rows // (2 * expert_total) - 1)
    slots = -(-capacity // 8) * 8
    chunk_rows = experts_dev * slots
    own_heads = -(-head_count // seq_size)
    own_cols = own_heads * HEAD_DIM
    all_cols = own_cols * seq_size

    tokens_all = lax.all_gather(tokens, "seq", axis=0, tiled=True)
    in_pieces = jnp.pad(
        attn_in.reshape(own_rows, 3, model_width), ((0, 0), (0, 0), (0, all_cols - model_width))
    ).reshape(own_rows, 3, seq_size, own_cols)
    in_pieces = in_pieces.transpose(2, 0, 1, 3).reshape(seq_size, own_rows, 3 * own_cols)
    small = jnp.concatenate([gain_attn[:, None], gain_ffn[:, None], router], axis=1)
    packed = jnp.concatenate(
        [in_pieces, jnp.broadcast_to(small[None], (seq_size,) + small.shape)], axis=2
    )
    packed = lax.all_to_all(packed, "seq", split_axis=0, concat_axis=0, tiled=True)
    packed = lax.all_gather(
        packed.reshape(seq_size * own_rows, -1), "exp", axis=0, tiled=True
    )
    w_own = packed[:, : 3 * own_cols]
    gain_one = packed[:, 3 * own_cols]
    gain_two = packed[:, 3 * own_cols + 1]
    w_router = packed[:, 3 * own_cols + 2 :]
    w_output = lax.all_gather(attn_out, ("exp", "seq"), axis=0, tiled=True)

    flat_ids = expert_ids.reshape(-1)
    id_table = (flat_ids[:, None] == jnp.arange(expert_total, dtype=jnp.int32)[None, :]).astype(
        jnp.int32
    )
    slot_rank = jnp.sum((jnp.cumsum(id_table, axis=0) - id_table) * id_table, axis=1)
    position = flat_ids * slots + slot_rank
    other_ids = expert_ids[:, ::-1].reshape(-1, 1).astype(jnp.bfloat16)
    upstream_rows = jnp.concatenate(
        [
            jnp.repeat(cotangent, 2, axis=0),
            jnp.pad(other_ids, ((0, 0), (0, 127))),
        ],
        axis=1,
    )

    def dispatch(values):
        sent = jnp.zeros((exp_size * chunk_rows, values.shape[1]), jnp.bfloat16)
        sent = sent.at[position].set(values).reshape(exp_size, chunk_rows, values.shape[1])
        received = lax.all_to_all(sent, "exp", split_axis=0, concat_axis=0, tiled=True)
        return lax.all_gather(received, "seq", axis=0, tiled=True).reshape(
            seq_size * exp_size, experts_dev, slots, values.shape[1]
        )

    upstream_all = dispatch(upstream_rows)

    inputs = tokens.astype(jnp.float32)
    inputs_all = tokens_all.astype(jnp.float32)
    normed_all, inverse_all = norm_forward(inputs_all, gain_one)
    normed_all_low = normed_all.astype(jnp.bfloat16)
    qkv_own = jnp.dot(normed_all_low, w_own, preferred_element_type=jnp.float32).astype(
        jnp.bfloat16
    )
    attended_own = attend(qkv_own, segments)
    attended_low = lax.all_to_all(
        attended_own.reshape(seq_size, tok_rows, own_cols),
        "seq",
        split_axis=0,
        concat_axis=0,
        tiled=True,
    )
    attended_low = attended_low.transpose(1, 0, 2).reshape(tok_rows, all_cols)[:, :model_width]
    hidden_state = inputs + jnp.dot(attended_low, w_output, preferred_element_type=jnp.float32)
    normed_two, inverse_two = norm_forward(hidden_state, gain_two)
    routed_low = normed_two.astype(jnp.bfloat16)
    all_rows = dispatch(jnp.repeat(routed_low, 2, axis=0))
    logits = jnp.dot(routed_low, w_router, preferred_element_type=jnp.float32)
    chosen = (
        expert_ids[:, :, None] == jnp.arange(expert_total, dtype=jnp.int32)[None, None, :]
    ).astype(jnp.float32)
    picked = jnp.sum(chosen * logits[:, None, :], axis=2)
    gate_values = jax.nn.softmax(picked, axis=-1)

    values = []
    backs = []
    in_grads = []
    out_grads = []
    row_count = seq_size * exp_size * slots
    for local_expert in range(experts_dev):
        rows = all_rows[:, local_expert].reshape(row_count, model_width)
        upstream_ext = upstream_all[:, local_expert].reshape(row_count, -1)
        row_logits = jnp.dot(rows, w_router, preferred_element_type=jnp.float32)
        expert_range = jnp.arange(expert_total, dtype=jnp.int32)[None, :]
        here = expert_range == exp_index * experts_dev + local_expert
        there = expert_range == upstream_ext[:, model_width : model_width + 1].astype(jnp.int32)
        logit_here = jnp.sum(jnp.where(here, row_logits, 0.0), axis=1, keepdims=True)
        logit_there = jnp.sum(jnp.where(there, row_logits, 0.0), axis=1, keepdims=True)
        top = jnp.maximum(logit_here, logit_there)
        raised = jnp.exp(logit_here - top)
        row_gates = raised / (raised + jnp.exp(logit_there - top))
        row_grads = (row_gates * upstream_ext[:, :model_width].astype(jnp.float32)).astype(
            jnp.bfloat16
        )
        pre_act = jnp.dot(rows, expert_in[local_expert], preferred_element_type=jnp.float32)
        activated, gelu_back = jax.vjp(jax.nn.gelu, pre_act)
        activated_low = activated.astype(jnp.bfloat16)
        values.append(
            jnp.dot(activated_low, expert_out[local_expert], preferred_element_type=jnp.float32)
        )
        hidden_grad = contract_cols(row_grads, expert_out[local_expert])
        pre_low = gelu_back(hidden_grad)[0].astype(jnp.bfloat16)
        backs.append(contract_cols(pre_low, expert_in[local_expert]))
        out_grads.append(contract_rows(activated_low, row_grads))
        in_grads.append(contract_rows(rows, pre_low))
    grad_expert_in = jnp.stack(in_grads, axis=0)
    grad_expert_out = jnp.stack(out_grads, axis=0)

    def give_back(pieces):
        stacked = jnp.stack(
            [
                piece.astype(jnp.bfloat16).reshape(seq_size, exp_size, slots, model_width)
                for piece in pieces
            ],
            axis=2,
        ).reshape(seq_size * exp_size, chunk_rows, model_width)
        own = lax.psum_scatter(stacked, "seq", scatter_dimension=0, tiled=True)
        own = lax.all_to_all(own, "exp", split_axis=0, concat_axis=0, tiled=True)
        return (
            own.reshape(-1, model_width)[position]
            .astype(jnp.float32)
            .reshape(tok_rows, 2, model_width)
        )

    expert_float = give_back(values)
    back_float = give_back(backs)
    mixed = hidden_state + jnp.sum(gate_values[:, :, None] * expert_float, axis=1)
    upstream = cotangent.astype(jnp.float32)
    gate_grad = jnp.sum(upstream[:, None, :] * expert_float, axis=2)
    picked_grad = gate_values * (
        gate_grad - jnp.sum(gate_values * gate_grad, axis=1, keepdims=True)
    )
    logit_grad = jnp.sum(chosen * picked_grad[:, :, None], axis=1)
    router_grad = jnp.dot(routed_low.astype(jnp.float32).T, logit_grad, precision=HIGHEST)
    routed_grad = jnp.dot(logit_grad, w_router.astype(jnp.float32).T, precision=HIGHEST)
    routed_grad = routed_grad + jnp.sum(back_float, axis=1)
    state_grad, gain_two_grad = norm_backward(hidden_state, inverse_two, gain_two, routed_grad)
    state_grad = state_grad + upstream
    state_low = state_grad.astype(jnp.bfloat16)

    state_all = lax.all_gather(state_low, "seq", axis=0, tiled=True)
    output_grad = contract_rows(attended_low, state_low).astype(jnp.bfloat16)
    output_grad = lax.psum_scatter(
        output_grad, ("exp", "seq"), scatter_dimension=0, tiled=True
    ).astype(jnp.float32)
    w_output_own = lax.dynamic_slice_in_dim(
        jnp.pad(w_output, ((0, all_cols - model_width), (0, 0))), seq_index * own_cols, own_cols
    )
    attended_grad = contract_cols(state_all, w_output_own).astype(jnp.bfloat16)
    qkv_grad = attend_back(qkv_own, attended_grad, segments)
    normed_part = contract_cols(qkv_grad, w_own)
    normed_grad = lax.psum_scatter(
        normed_part.astype(jnp.bfloat16), "seq", scatter_dimension=0, tiled=True
    ).astype(jnp.float32)
    weight_part = contract_rows(normed_all_low, qkv_grad)
    gain_one_part = jnp.sum(normed_part * inputs_all * inverse_all, axis=0)
    grad_pack = jnp.concatenate(
        [weight_part, gain_one_part[:, None], gain_two_grad[:, None], router_grad], axis=1
    ).astype(jnp.bfloat16)
    grad_pack = lax.all_to_all(
        grad_pack.reshape(exp_size, seq_size * own_rows, -1),
        "exp",
        split_axis=0,
        concat_axis=0,
        tiled=True,
    )
    grad_pack = jnp.sum(grad_pack.astype(jnp.float32), axis=0)
    grad_pack = lax.all_to_all(
        grad_pack.reshape(seq_size, own_rows, -1), "seq", split_axis=0, concat_axis=0, tiled=True
    )
    weight_grad = grad_pack[:, :, : 3 * own_cols].reshape(seq_size, own_rows, 3, own_cols)
    weight_grad = weight_grad.transpose(1, 2, 0, 3).reshape(own_rows, 3, all_cols)
    weight_grad = weight_grad[:, :, :model_width].reshape(own_rows, 3 * model_width)
    small_grad = jnp.sum(grad_pack[:, :, 3 * own_cols :], axis=0)

    first = seq_index * tok_rows
    inverse_one = lax.dynamic_slice_in_dim(inverse_all, first, tok_rows)
    input_part, _ = norm_backward(inputs, inverse_one, gain_one, normed_grad)
    input_grad = state_grad + input_part
    return (
        mixed.astype(jnp.bfloat16),
        input_grad,
        small_grad[:, 0],
        weight_grad,
        output_grad,
        small_grad[:, 1],
        small_grad[:, 2:],
        grad_expert_in,
        grad_expert_out,
    )


def solution(mesh):
    return jax.shard_map(
        on_device,
        mesh=mesh,
        in_specs=(
            P(("exp", "seq"), None),
            P("exp"),
            P(("exp", "seq"), None),
            P(("exp", "seq")),
            P(("exp", "seq"), None),
            P(("exp", "seq"), None),
            P(("exp", "seq")),
            P(("exp", "seq"), None),
            P("exp", None, "seq"),
            P("exp", "seq", None),
            P(("exp", "seq"), None),
        ),
        out_specs=(
            P(("exp", "seq"), None),
            P(("exp", "seq"), None),
            P(("exp", "seq")),
            P(("exp", "seq"), None),
            P(("exp", "seq"), None),
            P(("exp", "seq")),
            P(("exp", "seq"), None),
            P("exp", None, "seq"),
            P("exp", "seq", None),
        ),
        check_vma=False,
    )
```

time: 971 us -> 680 us (0.70)
  blocking collectives: 185 us -> 48.3 us
  matrix products: 129 us -> 62.2 us
  local copies, waits for them, and re-layouts: 96.9 us -> 39.8 us
  waiting for transfers between devices: 478 us -> 421 us
  Pallas kernels: 0 us -> 17.4 us
  starting transfers between devices: 9.29 us -> 26.4 us
    unnamed x17 -> x9, waiting for transfers between devices: 110 us -> 1.49 us
    unnamed x2 -> x0, blocking collectives: 81.5 us -> none
    all_gather x1, blocking collectives: 68.4 us -> 10.9 us  [on_device(): lax.all_gather(packed.reshape(seq_size * own_rows, -1), 'exp', axis=0, ti...]
    all_gather x5, waiting for transfers between devices: 164 us -> 209 us  [the longest x2 121 us: dispatch(): lax.all_gather(received, 'seq', axis=0, tiled=True)]
    unnamed x346 -> x108, local copies, waits for them, and re-layouts: 36.4 us -> 6.17 us
    dot_general x30 -> x6, matrix products: 49.4 us -> 22.7 us  [contract_rows(): lax.dot_general(first_operand, second_operand, (((0,), (0,)), ((), ())),...]
    reduce_scatter x7 -> x3, waiting for transfers between devices: 178 us -> 153 us  [the longest x2 121 us: give_back(): own = lax.psum_scatter(stacked, 'seq', scatter_dimension=0, tiled=True)]
    dot_general x30 -> x6, matrix products: 40.3 us -> 16.3 us  [contract_cols(): lax.dot_general(first_operand, second_operand, (((1,), (1,)), ((), ())),...]
  transfers between devices with their start and end apart: 17 -> 15, of which waited for: 12 -> 12; matrix products, arithmetic and copies ran while one was open for 23% -> 16% of each run, Pallas kernels for 0% -> 3%
where the time goes in v1:
time: 680 us; the launch traced here: 672 us
  waiting for transfers between devices  421 us (62%)
  matrix products  62.2 us (9%)
  blocking collectives  48.3 us (7%)
  other arithmetic  41.9 us (6%)
  local copies, waits for them, and re-layouts  39.8 us (6%)
  starting transfers between devices  26.4 us (4%)
  Pallas kernels  17.4 us (3%)
  between operations  15.3 us (2%)
    all_gather x2, waiting for transfers between devices, dispatch(): lax.all_gather(received, 'seq', axis=0, tiled=True)  121 us
    reduce_scatter x2, waiting for transfers between devices, give_back(): own = lax.psum_scatter(stacked, 'seq', scatter_dimension=0, tiled=True)  121 us
    all_gather x1, waiting for transfers between devices, on_device(): w_output = lax.all_gather(attn_out, ('exp', 'seq'), axis=0, tiled=True)  42.2 us
    reduce_scatter x1, waiting for transfers between devices, on_device(): lax.psum_scatter(output_grad, ('exp', 'seq'), scatter_dimension=0, tiled=...  38.4 us
    all_to_all x2, blocking collectives, dispatch(): lax.all_to_all(sent, 'exp', split_axis=0, concat_axis=0, tiled=True)  37.3 us
    reduce_scatter x1, waiting for transfers between devices, on_device(): lax.psum_scatter(normed_part.astype(jnp.bfloat16), 'seq', scatter_dimensi...  32.5 us
    all_gather x1, waiting for transfers between devices, on_device(): state_all = lax.all_gather(state_low, 'seq', axis=0, tiled=True)  31.3 us
    dot_general x6, matrix products, contract_rows(): lax.dot_general(first_operand, second_operand, (((0,), (0,)), ((), ())),...  22.7 us
  transfers between devices with their start and end apart: 15, of which 12 were waited for; matrix products, arithmetic and copies ran while one was open for 16% of the time, Pallas kernels for 3%

profile of v1, /device:TPU:0, one launch (start us, length us, event | category | flops | bytes accessed | tf_op | source)
XLA Modules:
  0.0 672.2 jit_solution(594303411095500107)
XLA Ops:
  11.5 6.3 all-to-all-start
  20.2 3.8 all-to-all-done
  24.0 10.9 %all_gather.19 = bf16[768,594]{1,0:T(8,128)(2,1)S(1)} all-gather(bf16[96,594]{1,0:T(8,128)(2,1)S(1)} %bitcast.158), channel_id=1, replica_groups=mesh['exp'=8,'seq'=4] {'exp'}, dimensions={0}, use_global_device_ids=true | all-gather | bytes 1026432 | tf_op jit(solution)/shard_map/all_gather | solution.py:179
  35.2 14.6 %all-gather.6.cloned.1.call-done = bf16[1024,768]{1,0:T(8,128)(2,1)} async-done(((bf16[256,768]{1,0:T(8,128)(2,1)}), bf16[1024,768]{1,0:T(8,128)(2,1)}) %all-gather.6.cloned.1.call-update) | async-done | bytes 1572880 | tf_op jit(solution)/shard_map/all_gather | solution.py:169
  51.7 2.9 convolution_convert_fusion.4.qkv_ref
  54.5 6.0 shard_map.178
  61.5 3.5 all-to-all-start.1
  66.8 42.2 %all-gather.8.cloned.1.call-done = bf16[768,768]{1,0:T(8,128)(2,1)} async-done(((bf16[24,768]{1,0:T(8,128)(2,1)}), bf16[768,768]{1,0:T(8,128)(2,1)}) %all-gather.8.cloned.1.call-update) | async-done | bytes 1179664 | tf_op jit(solution)/shard_map/all_gather | solution.py:186
  114.4 3.5 scatter_custom_fusion
  117.9 17.8 %all_to_all.40 = bf16[8,80,768]{2,1,0:T(8,128)(2,1)} all-to-all(bf16[8,80,768]{2,1,0:T(8,128)(2,1)S(1)} %bitcast.140), channel_id=1, replica_groups=mesh['exp'=8,'seq'=4] {'exp'}, dimensions={0} | all-to-all | bytes 1966080 | tf_op jit(solution)/shard_map/all_to_all | solution.py:206
  137.8 3.4 scatter_custom_fusion.1
  141.2 19.5 %all_to_all.41 = bf16[8,80,896]{2,1,0:T(8,128)(2,1)} all-to-all(bf16[8,80,896]{2,1,0:T(8,128)(2,1)S(1)} %bitcast.137), channel_id=1, replica_groups=mesh['exp'=8,'seq'=4] {'exp'}, dimensions={0} | all-to-all | bytes 2293760 | tf_op jit(solution)/shard_map/all_to_all | solution.py:206
  161.1 49.3 %all-gather.10.cloned.1.call-done = bf16[32,80,768]{2,1,0:T(8,128)(2,1)} async-done(((bf16[8,80,768]{2,1,0:T(8,128)(2,1)}), bf16[32,80,768]{2,1,0:T(8,128)(2,1)}) %all-gather.10.cloned.1.call-update) | async-done | bytes 3932176 | tf_op jit(solution)/shard_map/all_gather | solution.py:207
  210.4 2.5 fusion.85
  218.1 2.5 convolution_convert_fusion.2
  220.6 2.5 convolution_convert_fusion.3
  223.1 2.2 pad_maximum_fusion.2
  225.9 71.7 %all-gather.12.cloned.1.call-done = bf16[32,80,896]{2,1,0:T(8,128)(2,1)} async-done(((bf16[8,80,896]{2,1,0:T(8,128)(2,1)}), bf16[32,80,896]{2,1,0:T(8,128)(2,1)}) %all-gather.12.cloned.1.call-update) | async-done | bytes 4587536 | tf_op jit(solution)/shard_map/all_gather | solution.py:207
  297.7 2.9 fusion.84
  301.1 3.6 select_reduce_fusion
  306.5 3.9 fusion.13
  314.0 3.9 fusion.6
  319.6 2.3 pad_maximum_fusion.3
  322.0 49.0 %reduce-scatter.5.cloned.1.call-done = bf16[8,80,768]{2,1,0:T(8,128)(2,1)} async-done(((bf16[32,80,768]{2,1,0:T(8,128)(2,1)}), bf16[8,80,768]{2,1,0:T(8,128)(2,1)}) %reduce-scatter.5.cloned.1.call-update) | async-done | bytes 983056 | tf_op jit(solution)/shard_map/reduce_scatter | solution.py:282
  371.0 3.7 all-to-all-start.3
  374.7 71.5 %reduce-scatter.7.cloned.1.call-done = bf16[8,80,768]{2,1,0:T(8,128)(2,1)} async-done(((bf16[32,80,768]{2,1,0:T(8,128)(2,1)}), bf16[8,80,768]{2,1,0:T(8,128)(2,1)}) %reduce-scatter.7.cloned.1.call-update) | async-done | bytes 983056 | tf_op jit(solution)/shard_map/reduce_scatter | solution.py:282
  446.2 4.2 all-to-all-start.5
  453.3 2.7 gather_fusion
  456.0 9.1 %all-to-all-done.5 = bf16[8,80,768]{2,1,0:T(8,128)(2,1)} async-done(((bf16[8,80,768]{2,1,0:T(8,128)(2,1)}), bf16[8,80,768]{2,1,0:T(8,128)(2,1)}, u32[]{:S(2)}, u32[]{:S(2)}) %all-to-all-start.5) | async-done | bytes 983072 | tf_op jit(solution)/shard_map/all_to_all | solution.py:283
  465.2 4.4 gather_fusion.1
  469.6 3.0 reshape.378
  474.5 5.2 multiply_reduce_fusion
  479.8 4.2 reduce_sum.196
  484.0 2.8 multiply_reduce_fusion.2
  488.3 2.5 convolution_convert_fusion.5
  492.8 31.3 %all-gather.14.cloned.1.call-done = bf16[1024,768]{1,0:T(8,128)(2,1)} async-done(((bf16[256,768]{1,0:T(8,128)(2,1)}), bf16[1024,768]{1,0:T(8,128)(2,1)}) %all-gather.14.cloned.1.call-update) | async-done | bytes 1572880 | tf_op jit(solution)/shard_map/all_gather | solution.py:306
  526.4 11.4 %shard_map.179 = bf16[1024,576]{1,0:T(8,128)(2,1)S(1)} custom-call(bf16[1024,576]{1,0:T(8,128)(2,1)S(1)} %convolution_convert_fusion.4.qkv_ref, bf16[1024,192]{1,0:T(8,128)(2,1)S(1)} %copy.198.grad_ref, s32[1024,1]{1,0:T(8,128)S(1)} %copy.183.col_ref, s32[1,1024]{1,0:T(1,128)S(1)} %bitcast.126), custom_call_target="tpu_custom_call" | custom-call | flops 1811939328 | bytes 3538944 | tf_op jit(solution)/shard_map/pallas_call | solution.py:126
  537.9 2.9 fusion.18
  540.9 6.1 convolution_bitcast_fusion
  547.0 3.2 convolution_bitcast_fusion.2
  556.6 3.6 all-to-all-start.6
  560.2 4.9 convolution_bitcast_fusion.3
  565.1 3.9 convolution_bitcast_fusion.1
  569.0 5.9 all-to-all-done.6
  575.8 3.4 all-to-all-start.7
  579.2 7.6 %pad_maximum_fusion = (f32[2,768,768]{2,1,0:T(8,128)}, f32[2,768,768]{2,1,0:T(8,128)}) fusion(f32[1,768,768]{2,1,0:T(8,128)S(1)} %copy-done.11, f32[1,768,768]{2,1,0:T(8,128)} %convolution_bitcast_fusion.3, f32[1,768,768]{2,1,0:T(8,128)} %convolution_bitcast_fusion, f32[1,768,768]{2,1,0:T(8,128)} %convolution_bitcast_fusion.1), kind=kLoop, calls=%fused_computation.11 | loop fusion | flops 2359296 | bytes 18874368 | tf_op jit(solution)/shard_map/stack | solution.py:271
  586.8 38.4 %reduce-scatter.11.cloned.1.call-done = bf16[24,768]{1,0:T(8,128)(2,1)} async-done(((bf16[768,768]{1,0:T(8,128)(2,1)}), bf16[24,768]{1,0:T(8,128)(2,1)}) %reduce-scatter.11.cloned.1.call-update) | async-done | bytes 36880 | tf_op jit(solution)/shard_map/reduce_scatter | solution.py:308
  629.3 32.5 %reduce-scatter.9.cloned.1.call-done = bf16[256,768]{1,0:T(8,128)(2,1)} async-done(((bf16[1024,768]{1,0:T(8,128)(2,1)}), bf16[256,768]{1,0:T(8,128)(2,1)}) %reduce-scatter.9.cloned.1.call-update) | async-done | bytes 393232 | tf_op jit(solution)/shard_map/reduce_scatter | solution.py:317
  (214 shorter events, 57.7 us)
Async XLA Ops:
  7.2 12.8 %copy-start = (s32[1024]{0:T(1024)S(1)}, s32[1024]{0:T(1024)}, u32[]{:S(2)}) copy-start(s32[1024]{0:T(1024)} %param.12) | copy-start | bytes 12292
  7.2 42.7 %all-gather.6.cloned.1.call-start = ((), (), s32[]{:S(2)}) async-start(), calls=%async_computation.12 | async-start | bytes 1966080 | tf_op jit(solution)/shard_map/all_gather | solution.py:169
  7.9 101.1 %all-gather.8.cloned.1.call-start = ((), (), s32[]{:S(2)}) async-start(), calls=%async_computation.13 | async-start | bytes 1216512 | tf_op jit(solution)/shard_map/all_gather | solution.py:186
  11.5 12.4 %all-to-all-start = ((bf16[4,24,594]{2,1,0:T(8,128)(2,1)}), bf16[4,24,594]{2,1,0:T(8,128)(2,1)S(1)}, u32[]{:S(2)}, u32[]{:S(2)}) async-start(bf16[4,24,594]{2,1,0:T(8,128)(2,1)} %pad_maximum_fusion.5), calls=%async_computation | async-start | bytes 245760 | tf_op jit(solution)/shard_map/all_to_all | solution.py:178
  34.9 16.7 %copy-start.14 = (bf16[768,594]{1,0:T(8,128)(2,1)}, bf16[768,594]{1,0:T(8,128)(2,1)S(1)}, u32[]{:S(2)}) copy-start(bf16[768,594]{1,0:T(8,128)(2,1)S(1)} %all_gather.19) | copy-start | bytes 2737156
  54.5 54.5 %copy-start.12 = (bf16[256,768]{1,0:T(8,128)(2,1)S(1)}, bf16[256,768]{1,0:T(8,128)(2,1)}, u32[]{:S(2)}) copy-start(bf16[256,768]{1,0:T(8,128)(2,1)} %param.11) | copy-start | bytes 1179652
  61.5 47.5 %all-to-all-start.1 = ((bf16[4,256,192]{1,2,0:T(8,128)(2,1)}), bf16[4,256,192]{1,2,0:T(8,128)(2,1)S(1)}, u32[]{:S(2)}, u32[]{:S(2)}) async-start(bf16[4,256,192]{1,2,0:T(8,128)(2,1)} %copy.184), calls=%async_computation.1 | async-start | bytes 786432 | tf_op jit(solution)/shard_map/all_to_all | solution.py:221
  65.0 145.4 %all-gather.10.cloned.1.call-start = ((), (), s32[]{:S(2)}) async-start(), calls=%async_computation.14 | async-start | bytes 4915200 | tf_op jit(solution)/shard_map/all_gather | solution.py:207
  109.0 4.2 copy-start.17
  114.4 21.4 %copy-start.34 = (s32[256,2]{0,1:T(2,128)S(1)}, s32[256,2]{0,1:T(2,128)}, u32[]{:S(2)}) copy-start(s32[256,2]{0,1:T(2,128)} %param.13) | copy-start | bytes 6148
  114.4 21.8 %copy-start.16 = (bf16[256,768]{1,0:T(8,128)(2,1)S(1)}, bf16[256,768]{1,0:T(8,128)(2,1)}, u32[]{:S(2)}) copy-start(bf16[256,768]{1,0:T(8,128)(2,1)} %param.21) | copy-start | bytes 1179652
  135.7 161.9 %all-gather.12.cloned.1.call-start = ((), (), s32[]{:S(2)}) async-start(), calls=%async_computation.16 | async-start | bytes 5734400 | tf_op jit(solution)/shard_map/all_gather | solution.py:207
  160.8 210.2 %reduce-scatter.5.cloned.1.call-start = ((), (), s32[]{:S(2)}) async-start(), calls=%async_computation.15 | async-start | bytes 4915200 | tf_op jit(solution)/shard_map/reduce_scatter | solution.py:282
  225.4 220.9 %reduce-scatter.7.cloned.1.call-start = ((), (), s32[]{:S(2)}) async-start(), calls=%async_computation.17 | async-start | bytes 4915200 | tf_op jit(solution)/shard_map/reduce_scatter | solution.py:282
  297.7 8.8 %copy-start.52 = (f32[1280,768]{1,0:T(8,128)S(1)}, f32[1280,768]{1,0:T(8,128)}, u32[]{:S(2)}) copy-start(f32[1280,768]{1,0:T(8,128)} %copy-done.51) | copy-start | bytes 11796484
  300.5 5.9 copy-start.25
  300.5 13.0 %copy-start.23 = (bf16[32,1,40,896]{3,2,1,0:T(8,128)(2,1)}, bf16[32,1,40,896]{3,2,1,0:T(8,128)(2,1)S(1)}, u32[]{:S(2)}) copy-start(bf16[32,1,40,896]{3,2,1,0:T(8,128)(2,1)S(1)} %get-tuple-element.68) | copy-start | bytes 6881284
  300.5 4.2 copy-start.6
  300.8 5.7 copy-start.45
  306.4 4.0 copy-start.38
  306.5 7.1 %copy-start.36 = (f32[1280]{0:T(1024)}, f32[1280]{0:T(1024)S(1)}, u32[]{:S(2)}) copy-start(f32[1280]{0:T(1024)S(1)} %add_divide_fusion.1) | copy-start | bytes 15364
  306.5 5.3 copy-start.47
  371.0 75.2 %all-to-all-start.3 = ((bf16[8,80,768]{2,1,0:T(8,128)(2,1)}), bf16[8,80,768]{2,1,0:T(8,128)(2,1)S(1)}, u32[]{:S(2)}, u32[]{:S(2)}) async-start(bf16[8,80,768]{2,1,0:T(8,128)(2,1)} %reduce-scatter.5.cloned.1.call-done), calls=%async_computation.4 | async-start | bytes 1966080 | tf_op jit(solution)/shard_map/all_to_all | solution.py:283
  446.2 19.0 %all-to-all-start.5 = ((bf16[8,80,768]{2,1,0:T(8,128)(2,1)}), bf16[8,80,768]{2,1,0:T(8,128)(2,1)}, u32[]{:S(2)}, u32[]{:S(2)}) async-start(bf16[8,80,768]{2,1,0:T(8,128)(2,1)} %reduce-scatter.7.cloned.1.call-done), calls=%async_computation.7 | async-start | bytes 1966080 | tf_op jit(solution)/shard_map/all_to_all | solution.py:283
  450.4 73.7 %all-gather.14.cloned.1.call-start = ((), (), s32[]{:S(2)}) async-start(), calls=%async_computation.18 | async-start | bytes 1966080 | tf_op jit(solution)/shard_map/all_gather | solution.py:306
  474.5 9.5 %copy-start.4 = (f32[256,768]{1,0:T(8,128)S(1)}, f32[256,768]{1,0:T(8,128)}, u32[]{:S(2)}) copy-start(f32[256,768]{1,0:T(8,128)} %copy-done.3) | copy-start | bytes 2359300
  479.8 7.0 %copy-start.32 = (f32[256,16]{0,1:T(8,128)}, f32[256,16]{0,1:T(8,128)S(1)}, u32[]{:S(2)}) copy-start(f32[256,16]{0,1:T(8,128)S(1)} %select_reduce_fusion.4) | copy-start | bytes 49156
  479.8 7.0 %copy-start.43 = (f32[256]{0:T(256)S(1)}, f32[256]{0:T(256)}, u32[]{:S(2)}) copy-start(f32[256]{0:T(256)} %get-tuple-element.75) | copy-start | bytes 3076
  488.3 136.8 %reduce-scatter.11.cloned.1.call-start = ((), (), s32[]{:S(2)}) async-start(), calls=%async_computation.20 | async-start | bytes 1216512 | tf_op jit(solution)/shard_map/reduce_scatter | solution.py:308
  490.9 171.0 %reduce-scatter.9.cloned.1.call-start = ((), (), s32[]{:S(2)}) async-start(), calls=%async_computation.19 | async-start | bytes 1966080 | tf_op jit(solution)/shard_map/reduce_scatter | solution.py:317
  526.4 11.4 %copy-start.15 = (bf16[768,594]{1,0:T(8,128)(2,1)S(1)}, bf16[768,594]{1,0:T(8,128)(2,1)}, u32[]{:S(2)}) copy-start(bf16[768,594]{1,0:T(8,128)(2,1)} %copy-done.14) | copy-start | bytes 2737156
  526.4 11.4 %copy-start.30 = (bf16[1024,768]{1,0:T(8,128)(2,1)S(1)}, bf16[1024,768]{1,0:T(8,128)(2,1)}, u32[]{:S(2)}) copy-start(bf16[1024,768]{1,0:T(8,128)(2,1)} %all-gather.6.cloned.1.call-done) | copy-start | bytes 4718596
  526.4 11.4 %copy-start.41 = (f32[1024]{0:T(1024)S(1)}, f32[1024]{0:T(1024)}, u32[]{:S(2)}) copy-start(f32[1024]{0:T(1024)} %copy-done.40) | copy-start | bytes 12292
  540.8 6.1 copy-start.10
  540.9 6.1 copy-start.29
  547.0 3.8 copy-start.35
  547.0 4.2 copy-start.2
  547.0 4.2 copy-start.31
  554.9 5.3 copy-start.7
  556.6 18.4 %all-to-all-start.6 = ((bf16[8,96,594]{2,1,0:T(8,128)(2,1)}), bf16[8,96,594]{2,1,0:T(8,128)(2,1)S(1)}, u32[]{:S(2)}, u32[]{:S(2)}) async-start(bf16[8,96,594]{2,1,0:T(8,128)(2,1)} %pad_maximum_fusion.4), calls=%async_computation.9 | async-start | bytes 1966080 | tf_op jit(solution)/shard_map/all_to_all | solution.py:325
  560.2 4.9 copy-start.24
  560.2 4.9 copy-start.37
  560.2 4.9 copy-start.50
  565.1 14.0 %copy-start.11 = (f32[1,768,768]{2,1,0:T(8,128)S(1)}, f32[1,768,768]{2,1,0:T(8,128)}, u32[]{:S(2)}) copy-start(f32[1,768,768]{2,1,0:T(8,128)} %convolution_bitcast_fusion.2) | copy-start | bytes 7077892
  575.8 50.8 %all-to-all-start.7 = ((f32[4,24,594]{2,1,0:T(8,128)}), f32[4,24,594]{2,1,0:T(8,128)S(1)}, u32[]{:S(2)}, u32[]{:S(2)}) async-start(f32[4,24,594]{2,1,0:T(8,128)} %bitcast.156), calls=%async_computation.10 | async-start | bytes 491520 | tf_op jit(solution)/shard_map/all_to_all | solution.py:333
  586.8 75.1 %copy-start.13 = (bf16[256,768]{1,0:T(8,128)(2,1)S(1)}, bf16[256,768]{1,0:T(8,128)(2,1)}, u32[]{:S(2)}) copy-start(bf16[256,768]{1,0:T(8,128)(2,1)} %param.11) | copy-start | bytes 1179652
  586.8 76.3 %copy-start.20 = (f32[256,768]{1,0:T(8,128)S(1)}, f32[256,768]{1,0:T(8,128)}, u32[]{:S(2)}) copy-start(f32[256,768]{1,0:T(8,128)} %get-tuple-element.67) | copy-start | bytes 2359300
  586.8 76.3 %copy-start.42 = (f32[256,1]{0,1:T(1,128)S(1)}, f32[256,1]{0,1:T(1,128)}, u32[]{:S(2)}) copy-start(f32[256,1]{0,1:T(1,128)} %multiply_multiply_fusion.4) | copy-start | bytes 3076
  (20 other events, 47.1 us)
Sparse Core Ops, SparseCore 0:
  9.6 40.2 all-gather.5
  52.6 56.3 all-gather.7
  135.9 74.4 all-gather.9
  211.8 85.8 all-gather.11
  299.8 71.1 reduce-scatter.4
  373.2 72.9 reduce-scatter.6
  488.4 35.6 all-gather.13
  529.2 95.9 reduce-scatter.10
  627.4 34.3 reduce-scatter.8
